TPU v7x, 32 devices: a whole 2x2x4 slice. The times are simulated.
32 devices in a mesh: outer: 4 (over x, core), inner: 8 (over z, y).
Axes of the slice: x: 2, y: 2, z: 4, core: 2. Of those that a mesh axis runs over, the one named last changes fastest.
Arguments:
- vertex: float32 [8192, 1024], P(('outer', 'inner')), may hold values from -1.5 to 1.5
- vertex_state: float32 [8192], P(('outer', 'inner')), may hold values from 0.05 to 0.5
- context: float32 [8192, 1024], P(('outer', 'inner')), may hold values from -1.5 to 1.5
- context_state: float32 [8192], P(('outer', 'inner')), may hold values from 0.05 to 0.5
- edge_source: int32 [32, 1536], P(('outer', 'inner')), may hold values from 0 to 255
- edge_target: int32 [32, 1536], P(('outer', 'inner')), may hold values from 0 to 255
Outputs:
- vertex_out: float32 [8192, 1024], P(('outer', 'inner'))
- vertex_state_out: float32 [8192], P(('outer', 'inner'))
- context_out: float32 [8192, 1024], P(('outer', 'inner'))
- context_state_out: float32 [8192], P(('outer', 'inner'))
All inputs are finite; a program needn't handle non-finite values.
Results may differ from a plain program's by a relative error of at most 0.0019.
Values sent between devices are 32-bit elements; how exact they have to be, the bound alone decides.
A program may use at most 64 MiB of HBM per device.

v0:
```python
import jax
import jax.numpy as jnp
from jax import lax
from jax.sharding import PartitionSpec as P

ROUNDS = 3


def from_behind(array, axis, by):
    size = lax.axis_size(axis)
    return lax.ppermute(array, axis, [(i, (i + by) % size) for i in range(size)])


def edge_counts(source, target, row_count, block_rows):
    source_hot = (source[:, None] == jnp.arange(row_count, dtype=jnp.int32)[None, :]).astype(
        jnp.bfloat16
    )
    target_hot = (target[:, None] == jnp.arange(block_rows, dtype=jnp.int32)[None, :]).astype(
        jnp.bfloat16
    )
    return jnp.dot(source_hot.T, target_hot, preferred_element_type=jnp.float32)


def gradient(rows_b, block_b, source, target):
    scores = jnp.dot(rows_b, block_b.T, preferred_element_type=jnp.float32)
    prob = jax.nn.sigmoid(scores)
    counts = edge_counts(source, target, rows_b.shape[0], block_b.shape[0])
    return (prob / block_b.shape[0] - counts * (1.0 - prob)).astype(jnp.bfloat16)


def adagrad(weights, state, grad):
    state = state + jnp.mean(grad * grad, axis=1)
    return (weights - 0.1 * grad / jnp.sqrt(state)[:, None], state)


def body(vertex, vertex_state, context, context_state, edge_source, edge_target):
    rows, row_state = (vertex, vertex_state)
    block, block_state = (context, context_state)
    edges = edge_source.shape[1] // ROUNDS
    for step in range(ROUNDS):
        source = edge_source[0, step * edges : (step + 1) * edges]
        target = edge_target[0, step * edges : (step + 1) * edges]
        if step > 0:
            block, block_state = from_behind((block, block_state), "inner", 1)
        rows_b = rows.astype(jnp.bfloat16)
        block_b = block.astype(jnp.bfloat16)
        grad = gradient(rows_b, block_b, source, target)
        block_grad = jnp.dot(grad.T, rows_b, preferred_element_type=jnp.float32)
        rows_grad = jnp.dot(grad, block_b, preferred_element_type=jnp.float32)
        block, block_state = adagrad(block, block_state, block_grad)
        rows, row_state = adagrad(rows, row_state, rows_grad)
        if step == ROUNDS - 1:
            block, block_state = from_behind((block, block_state), "outer", 1)
    return (rows, row_state, block, block_state)


def solution(mesh):
    placed = (
        P(("outer", "inner"), None),
        P(("outer", "inner")),
        P(("outer", "inner"), None),
        P(("outer", "inner")),
        P(("outer", "inner"), None),
        P(("outer", "inner"), None),
    )
    return jax.shard_map(
        body,
        mesh=mesh,
        in_specs=placed,
        out_specs=(
            P(("outer", "inner"), None),
            P(("outer", "inner")),
            P(("outer", "inner"), None),
            P(("outer", "inner")),
        ),
        check_vma=False,
    )
```

profile of v0, /device:TPU:0, one launch (start us, length us, event | category | flops | bytes accessed | tf_op | source)
XLA Modules:
  0.0 80.7 jit_solution(6341440992005398119)
XLA Ops:
  0.6 0.7 fusion.45
  1.4 2.0 %fusion.7 = f32[256,256]{1,0:T(8,128)S(1)} fusion(f32[256,1024]{1,0:T(8,128)} %param.8, f32[256,1024]{1,0:T(8,128)} %param.6), kind=kOutput, calls=%fused_computation.13 | convolution fusion | flops 134938624 | bytes 2359296 | tf_op jit(solution)/shard_map/dot_general | solution.py:25
  3.4 0.5 fusion.12
  3.9 0.4 multiply_reduce_fusion.4
  4.3 0.7 copy-done.4
  5.0 0.1 copy-done
  5.1 0.3 divide_subtract_fusion.4
  5.4 3.0 %collective-permute-start = (f32[256,1024]{1,0:T(8,128)S(1)}, f32[256,1024]{1,0:T(8,128)S(1)}, u32[]{:S(2)}, u32[]{:S(2)}) collective-permute-start(f32[256,1024]{1,0:T(8,128)S(1)} %divide_subtract_fusion.4), channel_id=1, source_target_pairs={{0,1},{1,2},{2,3},{3,4},{4,5},{5,6},{6,7},{7,0},{8,9},{9,10},{10,1... | collective-permute-start | bytes 3145736 | tf_op jit(solution)/shard_map/ppermute | solution.py:11
  8.4 1.5 %collective-permute-start.1 = (f32[256]{0:T(256)S(1)}, f32[256]{0:T(256)S(1)}, u32[]{:S(2)}, u32[]{:S(2)}) collective-permute-start(f32[256]{0:T(256)S(1)} %get-tuple-element.11), channel_id=1, source_target_pairs={{0,1},{1,2},{2,3},{3,4},{4,5},{5,6},{6,7},{7,0},{8,9},{9,10},{10,1... | collective-permute-start | bytes 3080 | tf_op jit(solution)/shard_map/ppermute | solution.py:11
  9.9 0.4 multiply_reduce_fusion.5
  10.3 0.7 copy-done.2
  11.0 0.3 divide_subtract_fusion.5
  11.3 23.3 %collective-permute-done = f32[256,1024]{1,0:T(8,128)S(1)} collective-permute-done((f32[256,1024]{1,0:T(8,128)S(1)}, f32[256,1024]{1,0:T(8,128)S(1)}, u32[]{:S(2)}, u32[]{:S(2)}) %collective-permute-start) | collective-permute-done | bytes 1048608 | tf_op jit(solution)/shard_map/ppermute | solution.py:11
  34.6 0.4 fusion.9
  35.0 0.5 fusion.13
  35.4 0.4 multiply_reduce_fusion.2
  35.9 0.3 divide_subtract_fusion.2
  36.2 1.1 %collective-permute-start.3 = (f32[256]{0:T(256)S(1)}, f32[256]{0:T(256)S(1)}, u32[]{:S(2)}, u32[]{:S(2)}) collective-permute-start(f32[256]{0:T(256)S(1)} %get-tuple-element.9), channel_id=1, source_target_pairs={{0,1},{1,2},{2,3},{3,4},{4,5},{5,6},{6,7},{7,0},{8,9},{9,10},{10,1... | collective-permute-start | bytes 3080 | tf_op jit(solution)/shard_map/ppermute | solution.py:11
  37.3 0.4 multiply_reduce_fusion.3
  37.7 0.3 divide_subtract_fusion.3
  38.0 25.2 %collective-permute-done.2 = f32[256,1024]{1,0:T(8,128)S(1)} collective-permute-done((f32[256,1024]{1,0:T(8,128)S(1)}, f32[256,1024]{1,0:T(8,128)S(1)}, u32[]{:S(2)}, u32[]{:S(2)}) %collective-permute-start.2) | collective-permute-done | bytes 1048608 | tf_op jit(solution)/shard_map/ppermute | solution.py:11
  63.2 0.4 fusion.11
  63.6 0.5 fusion.14
  64.1 0.4 multiply_reduce_fusion
  64.5 0.3 divide_subtract_fusion
  64.9 1.4 %collective-permute-start.5 = (f32[256]{0:T(256)S(1)}, f32[256]{0:T(256)S(1)}, u32[]{:S(2)}, u32[]{:S(2)}) collective-permute-start(f32[256]{0:T(256)S(1)} %get-tuple-element.5), channel_id=1, source_target_pairs={{0,8},{8,16},{16,24},{24,0},{1,9},{9,17},{17,25},{25,1},{2,10},{10... | collective-permute-start | bytes 3080 | tf_op jit(solution)/shard_map/ppermute | solution.py:11
  66.3 0.4 multiply_reduce_fusion.1
  66.7 0.6 fusion.42
  67.2 1.2 %divide_subtract_fusion.1 = f32[256,1024]{1,0:T(8,128)} fusion(f32[256,1024]{1,0:T(8,128)S(1)} %divide_subtract_fusion.3, f32[256,1024]{1,0:T(8,128)S(1)} %get-tuple-element.27, f32[256]{0:T(256)S(1)} %get-tuple-element.6), kind=kLoop, calls=%fused_computation.23 | loop fusion | flops 786432 | bytes 3146752 | tf_op jit(solution)/shard_map/sub | solution.py:33
  68.5 10.7 %collective-permute-done.5 = f32[256]{0:T(256)S(1)} collective-permute-done((f32[256]{0:T(256)S(1)}, f32[256]{0:T(256)S(1)}, u32[]{:S(2)}, u32[]{:S(2)}) %collective-permute-start.5) | collective-permute-done | bytes 1056 | tf_op jit(solution)/shard_map/ppermute | solution.py:11
  79.1 1.0 %copy.12 = f32[256,1024]{1,0:T(8,128)} copy(f32[256,1024]{1,0:T(8,128)S(1)} %collective-permute-done.4) | data formatting | bytes 2097152
  80.1 0.6 copy.13
  (18 shorter events, 0.2 us)
Async XLA Ops:
  0.6 0.7 copy-start.3
  1.4 2.5 %copy-start.1 = (f32[256,1024]{1,0:T(8,128)S(1)}, f32[256,1024]{1,0:T(8,128)}, u32[]{:S(2)}) copy-start(f32[256,1024]{1,0:T(8,128)} %param.6) | copy-start | bytes 3145732
  3.9 1.2 %copy-start = (f32[256,1024]{1,0:T(8,128)S(1)}, f32[256,1024]{1,0:T(8,128)}, u32[]{:S(2)}) copy-start(f32[256,1024]{1,0:T(8,128)} %param.8) | copy-start | bytes 3145732
  4.3 0.7 copy-start.4
  5.4 29.2 %collective-permute-start = (f32[256,1024]{1,0:T(8,128)S(1)}, f32[256,1024]{1,0:T(8,128)S(1)}, u32[]{:S(2)}, u32[]{:S(2)}) collective-permute-start(f32[256,1024]{1,0:T(8,128)S(1)} %divide_subtract_fusion.4), channel_id=1, source_target_pairs={{0,1},{1,2},{2,3},{3,4},{4,5},{5,6},{6,7},{7,0},{8,9},{9,10},{10,1... | collective-permute-start | bytes 3145736 | tf_op jit(solution)/shard_map/ppermute | solution.py:11
  8.4 27.5 %collective-permute-start.1 = (f32[256]{0:T(256)S(1)}, f32[256]{0:T(256)S(1)}, u32[]{:S(2)}, u32[]{:S(2)}) collective-permute-start(f32[256]{0:T(256)S(1)} %get-tuple-element.11), channel_id=1, source_target_pairs={{0,1},{1,2},{2,3},{3,4},{4,5},{5,6},{6,7},{7,0},{8,9},{9,10},{10,1... | collective-permute-start | bytes 3080 | tf_op jit(solution)/shard_map/ppermute | solution.py:11
  10.3 0.7 copy-start.2
  36.2 27.1 %collective-permute-start.2 = (f32[256,1024]{1,0:T(8,128)S(1)}, f32[256,1024]{1,0:T(8,128)S(1)}, u32[]{:S(2)}, u32[]{:S(2)}) collective-permute-start(f32[256,1024]{1,0:T(8,128)S(1)} %divide_subtract_fusion.2), channel_id=1, source_target_pairs={{0,1},{1,2},{2,3},{3,4},{4,5},{5,6},{6,7},{7,0},{8,9},{9,10},{10,1... | collective-permute-start | bytes 3145736 | tf_op jit(solution)/shard_map/ppermute | solution.py:11
  36.2 28.3 %collective-permute-start.3 = (f32[256]{0:T(256)S(1)}, f32[256]{0:T(256)S(1)}, u32[]{:S(2)}, u32[]{:S(2)}) collective-permute-start(f32[256]{0:T(256)S(1)} %get-tuple-element.9), channel_id=1, source_target_pairs={{0,1},{1,2},{2,3},{3,4},{4,5},{5,6},{6,7},{7,0},{8,9},{9,10},{10,1... | collective-permute-start | bytes 3080 | tf_op jit(solution)/shard_map/ppermute | solution.py:11
  64.8 14.3 %collective-permute-start.4 = (f32[256,1024]{1,0:T(8,128)S(1)}, f32[256,1024]{1,0:T(8,128)S(1)}, u32[]{:S(2)}, u32[]{:S(2)}) collective-permute-start(f32[256,1024]{1,0:T(8,128)S(1)} %divide_subtract_fusion), channel_id=1, source_target_pairs={{0,8},{8,16},{16,24},{24,0},{1,9},{9,17},{17,25},{25,1},{2,10},{10... | collective-permute-start | bytes 3145736 | tf_op jit(solution)/shard_map/ppermute | solution.py:11
  64.9 14.3 %collective-permute-start.5 = (f32[256]{0:T(256)S(1)}, f32[256]{0:T(256)S(1)}, u32[]{:S(2)}, u32[]{:S(2)}) collective-permute-start(f32[256]{0:T(256)S(1)} %get-tuple-element.5), channel_id=1, source_target_pairs={{0,8},{8,16},{16,24},{24,0},{1,9},{9,17},{17,25},{25,1},{2,10},{10... | collective-permute-start | bytes 3080 | tf_op jit(solution)/shard_map/ppermute | solution.py:11
where the time goes:
time: 80.9 us; the launch traced here: 80.7 us
  waiting for transfers between devices  59.2 us (73%)
  starting transfers between devices  7.17 us (9%)
  matrix products  6.5 us (8%)
  local copies, waits for them, and re-layouts  3.74 us (5%)
  other arithmetic  3.21 us (4%)
  between operations  0.81 us (1%)
    ppermute x6, waiting for transfers between devices, from_behind(): lax.ppermute(array, axis, [(i, (i + by) % size) for i in range(size)])  59.2 us
    ppermute x6, starting transfers between devices, from_behind(): lax.ppermute(array, axis, [(i, (i + by) % size) for i in range(size)])  7.17 us
    unnamed x12, local copies, waits for them, and re-layouts  3.02 us
    dot_general x3, matrix products, gradient(): scores = jnp.dot(rows_b, block_b.T, preferred_element_type=jnp.float32)  2.68 us
    sub x6, other arithmetic, adagrad(): return (weights - 0.1 * grad / jnp.sqrt(state)[:, None], state)  2.6 us
  transfers between devices with their start and end apart: 6, of which 3 were waited for; matrix products, arithmetic and copies ran while one was open for 7% of the time, Pallas kernels for 0%

commit v1 on v0

v1 whole, which is shorter than its diff:
```python
import functools

import jax
import jax.numpy as jnp
from jax import lax
from jax.experimental import pallas as pl
from jax.experimental.pallas import tpu as pltpu
from jax.sharding import PartitionSpec as P

ROUNDS = 3
CHUNK = 32
DEPTH = 2

MESH = pl.DeviceIdType.MESH
BF16 = jnp.bfloat16
F32 = jnp.float32


def kernel(
    n_outer,
    n_inner,
    vertex,
    vertex_state,
    context,
    context_state,
    edge_source,
    edge_target,
    vertex_out,
    vertex_state_out,
    context_out,
    context_state_out,
    rows,
    rows_b,
    row_state,
    block,
    state,
    block_b,
    grads,
    counts,
    load_sem,
    send_sem,
    recv_sem,
    state_send_sem,
    state_recv_sem,
):
    pieces, chunk, width = context.shape
    row_count = rows.shape[0]
    block_rows = pieces * chunk
    edges = edge_source.shape[1] // ROUNDS
    hops = (ROUNDS - 1) * pieces

    i = lax.axis_index("inner")
    o = lax.axis_index("outer")
    right = {"inner": lax.rem(i + 1, n_inner)}
    left = {"inner": lax.rem(i + n_inner - 1, n_inner)}
    ahead = {"outer": lax.rem(o + 1, n_outer)}
    behind = {"outer": lax.rem(o + n_outer - 1, n_outer)}

    barrier = pltpu.get_barrier_semaphore()
    for neighbour in (left, right, behind, ahead):
        pl.semaphore_signal(barrier, inc=1, device_id=neighbour, device_id_type=MESH)

    load_rows = pltpu.make_async_copy(vertex, rows, load_sem.at[0])
    load_first = pltpu.make_async_copy(context.at[0], block.at[0], load_sem.at[1])
    load_rest = pltpu.make_async_copy(
        context.at[pl.ds(1, pieces - 1)], block.at[pl.ds(1, pieces - 1)], load_sem.at[2]
    )
    load_rows.start()
    load_first.start()
    load_rest.start()

    def hop(s):
        return pltpu.make_async_remote_copy(
            src_ref=block.at[s],
            dst_ref=block.at[s + pieces],
            send_sem=send_sem.at[s],
            recv_sem=recv_sem.at[s + pieces],
            device_id=right,
            device_id_type=MESH,
        )

    def state_hop(s):
        return pltpu.make_async_remote_copy(
            src_ref=state.at[s],
            dst_ref=state.at[s + pieces],
            send_sem=state_send_sem.at[s],
            recv_sem=state_recv_sem.at[s + pieces],
            device_id=right,
            device_id_type=MESH,
        )

    def leave(k):
        return pltpu.make_async_remote_copy(
            src_ref=block.at[hops + k],
            dst_ref=context_out.at[k],
            send_sem=send_sem.at[hops + k],
            recv_sem=recv_sem.at[hops + pieces + k],
            device_id=ahead,
            device_id_type=MESH,
        )

    def state_leave(k):
        return pltpu.make_async_remote_copy(
            src_ref=state.at[hops + k],
            dst_ref=state.at[hops + pieces + k],
            send_sem=state_send_sem.at[hops + k],
            recv_sem=state_recv_sem.at[hops + pieces + k],
            device_id=ahead,
            device_id_type=MESH,
        )

    def count(r):
        span = pl.ds(r * edges, edges)
        target_hot = (
            edge_target[:, span] == lax.broadcasted_iota(jnp.int32, (block_rows, edges), 0)
        ).astype(F32).astype(BF16)
        source_hot = (
            edge_source[:, span] == lax.broadcasted_iota(jnp.int32, (row_count, edges), 0)
        ).astype(F32).astype(BF16)
        counts[r] = lax.dot_general(
            target_hot, source_hot, (((1,), (1,)), ((), ())), preferred_element_type=F32
        ).reshape(pieces, chunk, row_count)

    def update_chunk(slot, r, k):
        held = block[slot]
        held_b = held.astype(BF16)
        block_b[k] = held_b
        scores = lax.dot_general(
            held_b, rows_b[...], (((1,), (1,)), ((), ())), preferred_element_type=F32
        )
        prob = 1.0 / (1.0 + jnp.exp(-scores))
        grad = (prob * (1.0 / block_rows) - counts[r, k] * (1.0 - prob)).astype(BF16)
        grads[k] = grad
        chunk_grad = jnp.dot(grad, rows_b[...], preferred_element_type=F32)
        place = lax.broadcasted_iota(jnp.int32, (chunk, block_rows), 0) + k * chunk
        lane = lax.broadcasted_iota(jnp.int32, (chunk, block_rows), 1)
        mine = place == lane
        total = jnp.sum(jnp.where(mine, state[slot], 0.0), axis=1, keepdims=True)
        total = total + jnp.sum(chunk_grad * chunk_grad, axis=1, keepdims=True) * (1.0 / width)
        block[slot] = held - chunk_grad * (0.1 * lax.rsqrt(total))
        state[slot] = jnp.sum(jnp.where(mine, total, 0.0), axis=0, keepdims=True)

    def update_rows():
        rows_grad = lax.dot_general(
            grads[...].reshape(block_rows, row_count),
            block_b[...].reshape(block_rows, width),
            (((0,), (0,)), ((), ())),
            preferred_element_type=F32,
        )
        total = row_state[...] + jnp.sum(rows_grad * rows_grad, axis=1, keepdims=True) * (
            1.0 / width
        )
        row_state[...] = total
        rows[...] = rows[...] - rows_grad * (0.1 * lax.rsqrt(total))
        rows_b[...] = rows[...].astype(BF16)

    eye = lax.broadcasted_iota(jnp.int32, (row_count, row_count), 0) == lax.broadcasted_iota(
        jnp.int32, (row_count, row_count), 1
    )
    row_state[...] = jnp.sum(jnp.where(eye, vertex_state[...], 0.0), axis=1, keepdims=True)
    for k in range(pieces):
        state[k] = context_state[...]
    count(0)
    load_rows.wait()
    rows_b[...] = rows[...].astype(BF16)
    load_first.wait()
    update_chunk(0, 0, 0)
    pl.semaphore_wait(barrier, 4)
    hop(0).start()
    state_hop(0).start()
    load_rest.wait()

    @pl.loop(1, pieces)
    def _(k):
        update_chunk(k, 0, k)

        @pl.when(k < DEPTH)
        def _():
            hop(k).start()
            state_hop(k).start()

    for r in range(1, ROUNDS):
        count(r)
    update_rows()

    for r in range(1, ROUNDS):

        @pl.loop(0, pieces)
        def _(k):
            s = (r - 1) * pieces + k
            hop(s).wait_send()
            state_hop(s).wait_send()

            @pl.when(s + DEPTH < hops)
            def _():
                hop(s + DEPTH).start()
                state_hop(s + DEPTH).start()

            hop(s).wait_recv()
            state_hop(s).wait_recv()
            update_chunk(s + pieces, r, k)
            if r == ROUNDS - 1:
                leave(k).start()
                state_leave(k).start()

        update_rows()

    store_rows = pltpu.make_async_copy(rows, vertex_out, load_sem.at[0])
    store_rows.start()
    vertex_state_out[...] = jnp.sum(jnp.where(eye, row_state[...], 0.0), axis=0, keepdims=True)

    @pl.loop(0, pieces)
    def _(k):
        leave(k).wait()
        state_leave(k).wait()

    context_state_out[...] = jnp.sum(state[pl.ds(hops + pieces, pieces)], axis=0)
    store_rows.wait()


def body(n_outer, n_inner, vertex, vertex_state, context, context_state, edge_source, edge_target):
    row_count, width = vertex.shape
    block_rows = context.shape[0]
    pieces = block_rows // CHUNK
    slots = ROUNDS * pieces
    whole = pl.BlockSpec(memory_space=pl.ANY)
    small = pl.BlockSpec(memory_space=pltpu.VMEM)
    vertex_out, vertex_state_out, context_out, context_state_out = pl.pallas_call(
        functools.partial(kernel, n_outer, n_inner),
        out_shape=(
            jax.ShapeDtypeStruct((row_count, width), F32),
            jax.ShapeDtypeStruct((1, row_count), F32),
            jax.ShapeDtypeStruct((pieces, CHUNK, width), F32),
            jax.ShapeDtypeStruct((1, block_rows), F32),
        ),
        in_specs=[whole, small, whole, small, small, small],
        out_specs=(whole, small, whole, small),
        scratch_shapes=[
            pltpu.VMEM((row_count, width), F32),
            pltpu.VMEM((row_count, width), BF16),
            pltpu.VMEM((row_count, 1), F32),
            pltpu.VMEM((slots, CHUNK, width), F32),
            pltpu.VMEM((slots + pieces, 1, block_rows), F32),
            pltpu.VMEM((pieces, CHUNK, width), BF16),
            pltpu.VMEM((pieces, CHUNK, row_count), BF16),
            pltpu.VMEM((ROUNDS, pieces, CHUNK, row_count), F32),
            pltpu.SemaphoreType.DMA((3,)),
            pltpu.SemaphoreType.DMA((slots,)),
            pltpu.SemaphoreType.DMA((slots + pieces,)),
            pltpu.SemaphoreType.DMA((slots,)),
            pltpu.SemaphoreType.DMA((slots + pieces,)),
        ],
        compiler_params=pltpu.CompilerParams(
            collective_id=0, has_side_effects=True, vmem_limit_bytes=32 * 1024 * 1024
        ),
        cost_estimate=pl.CostEstimate(
            flops=ROUNDS * 2 * row_count * block_rows * (3 * width + 512),
            bytes_accessed=16 * row_count * width,
            transcendentals=ROUNDS * row_count * block_rows,
        ),
    )(
        vertex,
        vertex_state.reshape(1, row_count),
        context.reshape(pieces, CHUNK, width),
        context_state.reshape(1, block_rows),
        edge_source,
        edge_target,
    )
    return (
        vertex_out,
        vertex_state_out.reshape(row_count),
        context_out.reshape(block_rows, width),
        context_state_out.reshape(block_rows),
    )


def solution(mesh):
    matrix = P(("outer", "inner"), None)
    vector = P(("outer", "inner"))
    return jax.shard_map(
        functools.partial(body, mesh.shape["outer"], mesh.shape["inner"]),
        mesh=mesh,
        in_specs=(matrix, vector, matrix, vector, matrix, matrix),
        out_specs=(matrix, vector, matrix, vector),
        check_vma=False,
    )
```

time: 80.9 us -> 67.1 us (0.83)
  waiting for transfers between devices: 59.2 us -> 0 us
  Pallas kernels: 0 us -> 58.6 us
  starting transfers between devices: 7.17 us -> 0 us
  matrix products: 6.5 us -> 0 us
  local copies, waits for them, and re-layouts: 3.74 us -> 7.58 us
  other arithmetic: 3.21 us -> 0 us
    ppermute x6 -> x0, waiting for transfers between devices: 59.2 us -> none  [from_behind(): lax.ppermute(array, axis, [(i, (i + by) % size) for i in range(size)])]
    pallas_call x0 -> x1, Pallas kernels: none -> 58.6 us  [body(): pl.pallas_call(functools.partial(kernel, n_outer, n_inner), out_shape=(ja...]
    ppermute x6 -> x0, starting transfers between devices: 7.17 us -> none  [from_behind(): lax.ppermute(array, axis, [(i, (i + by) % size) for i in range(size)])]
    dot_general x12 -> x0, matrix products: 6.5 us -> none  [the longest x3 2.68 us: gradient(): scores = jnp.dot(rows_b, block_b.T, preferred_element_type=jnp.float32)]
    unnamed x12 -> x16, local copies, waits for them, and re-layouts: 3.02 us -> 7.58 us
    sub x6 -> x0, other arithmetic: 2.6 us -> none  [adagrad(): return (weights - 0.1 * grad / jnp.sqrt(state)[:, None], state)]
  transfers between devices with their start and end apart: 6 -> 0, of which waited for: 3 -> 0; matrix products, arithmetic and copies ran while one was open for 7% -> 0% of each run, Pallas kernels for 0% -> 0%
where the time goes in v1:
time: 67.1 us; the launch traced here: 66.8 us
  Pallas kernels  58.6 us (87%)
  local copies, waits for them, and re-layouts  7.58 us (11%)
    pallas_call x1, Pallas kernels, body(): pl.pallas_call(functools.partial(kernel, n_outer, n_inner), out_shape=(ja...  58.6 us
    unnamed x16, local copies, waits for them, and re-layouts  7.58 us

profile of v1, /device:TPU:0, one launch (start us, length us, event | category | flops | bytes accessed | tf_op | source)
XLA Modules:
  0.0 66.8 jit_solution(885598713105232240)
XLA Ops:
  0.6 0.0 copy-start.5
  0.6 0.0 copy-start.4
  0.7 0.7 copy-done.5
  1.3 0.0 copy-done.4
  1.3 0.0 copy-start
  1.3 1.2 %copy-done = f32[256,1024]{1,0:T(8,128)S(1)} copy-done((f32[256,1024]{1,0:T(8,128)S(1)}, f32[256,1024]{1,0:T(8,128)}, u32[]{:S(2)}) %copy-start) | copy-done | bytes 1048600
  2.6 0.0 copy-start.1
  2.6 1.2 %copy-done.1 = f32[256,1024]{1,0:T(8,128)S(1)} copy-done((f32[256,1024]{1,0:T(8,128)S(1)}, f32[256,1024]{1,0:T(8,128)}, u32[]{:S(2)}) %copy-start.1) | copy-done | bytes 1048600
  3.8 0.0 copy-start.2
  3.8 0.7 %copy-done.2 = s32[1,1536]{1,0:T(1,128)S(1)} copy-done((s32[1,1536]{1,0:T(1,128)S(1)}, s32[1,1536]{1,0:T(1,128)}, u32[]{:S(2)}) %copy-start.2) | copy-done | bytes 6168
  4.5 0.0 copy-start.3
  4.5 0.7 %copy-done.3 = s32[1,1536]{1,0:T(1,128)S(1)} copy-done((s32[1,1536]{1,0:T(1,128)S(1)}, s32[1,1536]{1,0:T(1,128)}, u32[]{:S(2)}) %copy-start.3) | copy-done | bytes 6168
  5.2 58.6 %shard_map.93 = (f32[256,1024]{1,0:T(8,128)S(1)}, f32[1,256]{1,0:T(1,128)S(1)}, f32[8,32,1024]{2,1,0:T(8,128)S(1)}, f32[1,256]{1,0:T(1,128)S(1)}) custom-call(f32[256,1024]{1,0:T(8,128)S(1)} %copy-done, f32[1,256]{1,0:T(1,128)S(1)} %bitcast.10, f32[8,32,1024]{2,1,0:T(8,128)S(1)} %bitcast.9, f32[1,256]{1,0:T(1,128)S(1)} %bitcast.11, s32[1,1536]{1,0:T(1,128)S(1)} %copy-done.2, ...), custom_call_target="tpu_custom_call" | custom-call | flops 1409286144 | bytes 4194304 | tf_op jit(solution)/shard_map/pallas_call | solution.py:228
  63.7 1.0 %copy.14 = f32[256,1024]{1,0:T(8,128)} copy(f32[256,1024]{1,0:T(8,128)S(1)} %get-tuple-element.16) | data formatting | bytes 2097152
  64.7 0.6 copy.15
  65.3 1.0 %copy.16 = f32[256,1024]{1,0:T(8,128)} copy(f32[256,1024]{1,0:T(8,128)S(1)} %bitcast.6) | data formatting | bytes 2097152
  66.2 0.6 copy.17
Async XLA Ops:
  0.6 0.7 %copy-start.5 = (f32[256]{0:T(256)S(1)}, f32[256]{0:T(256)}, u32[]{:S(2)}) copy-start(f32[256]{0:T(256)} %param.9) | copy-start | bytes 3076
  0.6 0.7 %copy-start.4 = (f32[256]{0:T(256)S(1)}, f32[256]{0:T(256)}, u32[]{:S(2)}) copy-start(f32[256]{0:T(256)} %param.7) | copy-start | bytes 3076
  1.3 1.2 %copy-start = (f32[256,1024]{1,0:T(8,128)S(1)}, f32[256,1024]{1,0:T(8,128)}, u32[]{:S(2)}) copy-start(f32[256,1024]{1,0:T(8,128)} %vertex.1) | copy-start | bytes 3145732
  2.6 1.2 %copy-start.1 = (f32[256,1024]{1,0:T(8,128)S(1)}, f32[256,1024]{1,0:T(8,128)}, u32[]{:S(2)}) copy-start(f32[256,1024]{1,0:T(8,128)} %param.8) | copy-start | bytes 3145732
  3.8 0.7 %copy-start.2 = (s32[1,1536]{1,0:T(1,128)S(1)}, s32[1,1536]{1,0:T(1,128)}, u32[]{:S(2)}) copy-start(s32[1,1536]{1,0:T(1,128)} %edge_source.1) | copy-start | bytes 18436
  4.5 0.7 %copy-start.3 = (s32[1,1536]{1,0:T(1,128)S(1)}, s32[1,1536]{1,0:T(1,128)}, u32[]{:S(2)}) copy-start(s32[1,1536]{1,0:T(1,128)} %edge_target.1) | copy-start | bytes 18436

commit v2 on v1

--- a/solution.py
+++ b/solution.py
@@ -9,7 +9,7 @@
 
 ROUNDS = 3
 CHUNK = 32
-DEPTH = 2
+DEPTH = 4
 
 MESH = pl.DeviceIdType.MESH
 BF16 = jnp.bfloat16
@@ -20,16 +20,19 @@
     n_outer,
     n_inner,
     vertex,
+    vertex_state_in,
+    context,
+    context_state_in,
+    edge_source_in,
+    edge_target_in,
+    rows,
+    vertex_state_out,
+    context_out,
+    context_state_out,
     vertex_state,
-    context,
     context_state,
     edge_source,
     edge_target,
-    vertex_out,
-    vertex_state_out,
-    context_out,
-    context_state_out,
-    rows,
     rows_b,
     row_state,
     block,
@@ -46,7 +49,7 @@
     pieces, chunk, width = context.shape
     row_count = rows.shape[0]
     block_rows = pieces * chunk
-    edges = edge_source.shape[1] // ROUNDS
+    edges = edge_source_in.shape[1] // ROUNDS
     hops = (ROUNDS - 1) * pieces
 
     i = lax.axis_index("inner")
@@ -60,6 +63,19 @@
     for neighbour in (left, right, behind, ahead):
         pl.semaphore_signal(barrier, inc=1, device_id=neighbour, device_id_type=MESH)
 
+    small_loads = [
+        pltpu.make_async_copy(source, target, load_sem.at[3 + n])
+        for n, (source, target) in enumerate(
+            (
+                (edge_source_in, edge_source),
+                (edge_target_in, edge_target),
+                (vertex_state_in, vertex_state),
+                (context_state_in, context_state),
+            )
+        )
+    ]
+    for load in small_loads:
+        load.start()
     load_rows = pltpu.make_async_copy(vertex, rows, load_sem.at[0])
     load_first = pltpu.make_async_copy(context.at[0], block.at[0], load_sem.at[1])
     load_rest = pltpu.make_async_copy(
@@ -154,6 +170,8 @@
         rows[...] = rows[...] - rows_grad * (0.1 * lax.rsqrt(total))
         rows_b[...] = rows[...].astype(BF16)
 
+    for load in small_loads:
+        load.wait()
     eye = lax.broadcasted_iota(jnp.int32, (row_count, row_count), 0) == lax.broadcasted_iota(
         jnp.int32, (row_count, row_count), 1
     )
@@ -205,8 +223,6 @@
 
         update_rows()
 
-    store_rows = pltpu.make_async_copy(rows, vertex_out, load_sem.at[0])
-    store_rows.start()
     vertex_state_out[...] = jnp.sum(jnp.where(eye, row_state[...], 0.0), axis=0, keepdims=True)
 
     @pl.loop(0, pieces)
@@ -215,7 +231,18 @@
         state_leave(k).wait()
 
     context_state_out[...] = jnp.sum(state[pl.ds(hops + pieces, pieces)], axis=0)
-    store_rows.wait()
+
+
+def store_kernel(*refs):
+    sources, targets, sems = refs[:4], refs[4:8], refs[8]
+    copies = [
+        pltpu.make_async_copy(source, target, sems.at[n])
+        for n, (source, target) in enumerate(zip(sources, targets))
+    ]
+    for copy in copies:
+        copy.start()
+    for copy in copies:
+        copy.wait()
 
 
 def body(n_outer, n_inner, vertex, vertex_state, context, context_state, edge_source, edge_target):
@@ -223,20 +250,24 @@
     block_rows = context.shape[0]
     pieces = block_rows // CHUNK
     slots = ROUNDS * pieces
-    whole = pl.BlockSpec(memory_space=pl.ANY)
-    small = pl.BlockSpec(memory_space=pltpu.VMEM)
-    vertex_out, vertex_state_out, context_out, context_state_out = pl.pallas_call(
+    far = pl.BlockSpec(memory_space=pltpu.HBM)
+    near = pl.BlockSpec(memory_space=pltpu.VMEM)
+    shapes = (
+        (row_count, width),
+        (1, row_count),
+        (pieces, CHUNK, width),
+        (1, block_rows),
+    )
+    results = pl.pallas_call(
         functools.partial(kernel, n_outer, n_inner),
-        out_shape=(
-            jax.ShapeDtypeStruct((row_count, width), F32),
-            jax.ShapeDtypeStruct((1, row_count), F32),
-            jax.ShapeDtypeStruct((pieces, CHUNK, width), F32),
-            jax.ShapeDtypeStruct((1, block_rows), F32),
-        ),
-        in_specs=[whole, small, whole, small, small, small],
-        out_specs=(whole, small, whole, small),
+        out_shape=tuple(pltpu.VMEM(shape, F32) for shape in shapes),
+        in_specs=[far] * 6,
+        out_specs=(near,) * 4,
         scratch_shapes=[
-            pltpu.VMEM((row_count, width), F32),
+            pltpu.VMEM((1, row_count), F32),
+            pltpu.VMEM((1, block_rows), F32),
+            pltpu.VMEM(edge_source.shape, jnp.int32),
+            pltpu.VMEM(edge_target.shape, jnp.int32),
             pltpu.VMEM((row_count, width), BF16),
             pltpu.VMEM((row_count, 1), F32),
             pltpu.VMEM((slots, CHUNK, width), F32),
@@ -244,14 +275,14 @@
             pltpu.VMEM((pieces, CHUNK, width), BF16),
             pltpu.VMEM((pieces, CHUNK, row_count), BF16),
             pltpu.VMEM((ROUNDS, pieces, CHUNK, row_count), F32),
-            pltpu.SemaphoreType.DMA((3,)),
+            pltpu.SemaphoreType.DMA((7,)),
             pltpu.SemaphoreType.DMA((slots,)),
             pltpu.SemaphoreType.DMA((slots + pieces,)),
             pltpu.SemaphoreType.DMA((slots,)),
             pltpu.SemaphoreType.DMA((slots + pieces,)),
         ],
         compiler_params=pltpu.CompilerParams(
-            collective_id=0, has_side_effects=True, vmem_limit_bytes=32 * 1024 * 1024
+            collective_id=0, has_side_effects=True, vmem_limit_bytes=56 * 1024 * 1024
         ),
         cost_estimate=pl.CostEstimate(
             flops=ROUNDS * 2 * row_count * block_rows * (3 * width + 512),
@@ -266,6 +297,13 @@
         edge_source,
         edge_target,
     )
+    vertex_out, vertex_state_out, context_out, context_state_out = pl.pallas_call(
+        store_kernel,
+        out_shape=tuple(jax.ShapeDtypeStruct(shape, F32) for shape in shapes),
+        in_specs=[near] * 4,
+        out_specs=(far,) * 4,
+        scratch_shapes=[pltpu.SemaphoreType.DMA((4,))],
+    )(*results)
     return (
         vertex_out,
         vertex_state_out.reshape(row_count),

time: 67.1 us -> 65.2 us (0.972)
  local copies, waits for them, and re-layouts: 7.58 us -> 2.58 us
  Pallas kernels: 58.6 us -> 61.8 us
    unnamed x16 -> x8, local copies, waits for them, and re-layouts: 7.58 us -> 2.58 us
    pallas_call x1 -> x2, Pallas kernels: 58.6 us -> 61.8 us  [the longest x1 58.9 us: body(): pl.pallas_call(functools.partial(kernel, n_outer, n_inner), out_shape=tup...]
where the time goes in v2:
time: 65.2 us; the launch traced here: 65 us
  Pallas kernels  61.8 us (95%)
  local copies, waits for them, and re-layouts  2.58 us (4%)
    pallas_call x1, Pallas kernels, body(): pl.pallas_call(functools.partial(kernel, n_outer, n_inner), out_shape=tup...  58.9 us
    pallas_call x1, Pallas kernels, body(): pl.pallas_call(store_kernel, out_shape=tuple((jax.ShapeDtypeStruct(shape,...  2.9 us
    unnamed x8, local copies, waits for them, and re-layouts  2.58 us

profile of v2, /device:TPU:0, one launch (start us, length us, event | category | flops | bytes accessed | tf_op | source)
XLA Modules:
  0.0 65.0 jit_solution(4063178089780866655)
XLA Ops:
  0.6 58.9 %shard_map.93 = (f32[256,1024]{1,0:T(8,128)S(1)}, f32[1,256]{1,0:T(1,128)S(1)}, f32[8,32,1024]{2,1,0:T(8,128)S(1)}, f32[1,256]{1,0:T(1,128)S(1)}) custom-call(f32[256,1024]{1,0:T(8,128)} %vertex.1, f32[1,256]{1,0:T(1,128)} %bitcast.8, f32[8,32,1024]{2,1,0:T(8,128)} %bitcast.6, f32[1,256]{1,0:T(1,128)} %bitcast.9, s32[1,1536]{1,0:T(1,128)} %edge_source_in.1, ...), custom_call_target="tpu_custom_call" | custom-call | flops 1409286144 | bytes 4194304 | tf_op jit(solution)/shard_map/pallas_call | solution.py:261
  59.5 0.0 copy-start
  59.6 1.0 %copy-done = f32[256,1024]{1,0:T(8,128)} copy-done((f32[256,1024]{1,0:T(8,128)}, f32[256,1024]{1,0:T(8,128)S(1)}, u32[]{:S(2)}) %copy-start) | copy-done | bytes 1048600
  60.5 0.0 copy-start.1
  60.5 1.0 %copy-done.1 = f32[8,32,1024]{2,1,0:T(8,128)} copy-done((f32[8,32,1024]{2,1,0:T(8,128)}, f32[8,32,1024]{2,1,0:T(8,128)S(1)}, u32[]{:S(2)}) %copy-start.1) | copy-done | bytes 1048600
  61.5 0.0 copy-start.2
  61.6 0.0 copy-start.3
  61.6 0.6 copy-done.2
  62.1 0.0 copy-done.3
  62.1 2.9 %shard_map.94 = (f32[256,1024]{1,0:T(8,128)}, f32[1,256]{1,0:T(1,128)}, f32[8,32,1024]{2,1,0:T(8,128)}, f32[1,256]{1,0:T(1,128)}) custom-call(f32[256,1024]{1,0:T(8,128)} %copy-done, f32[1,256]{1,0:T(1,128)} %copy-done.2, f32[8,32,1024]{2,1,0:T(8,128)} %copy-done.1, f32[1,256]{1,0:T(1,128)} %copy-done.3), custom_call_target="tpu_custom_call" | custom-call | tf_op jit(solution)/shard_map/pallas_call | solution.py:300
Async XLA Ops:
  59.5 1.0 %copy-start = (f32[256,1024]{1,0:T(8,128)}, f32[256,1024]{1,0:T(8,128)S(1)}, u32[]{:S(2)}) copy-start(f32[256,1024]{1,0:T(8,128)S(1)} %get-tuple-element.12.refs_0_) | copy-start | bytes 3145732
  60.5 1.0 %copy-start.1 = (f32[8,32,1024]{2,1,0:T(8,128)}, f32[8,32,1024]{2,1,0:T(8,128)S(1)}, u32[]{:S(2)}) copy-start(f32[8,32,1024]{2,1,0:T(8,128)S(1)} %get-tuple-element.14.refs_2_) | copy-start | bytes 3145732
  61.5 0.6 copy-start.2
  61.6 0.6 copy-start.3

commit v3 on v2

--- a/solution.py
+++ b/solution.py
@@ -8,7 +8,7 @@
 from jax.sharding import PartitionSpec as P
 
 ROUNDS = 3
-CHUNK = 32
+CHUNK = 16
 DEPTH = 4
 
 MESH = pl.DeviceIdType.MESH
@@ -303,6 +303,7 @@
         in_specs=[near] * 4,
         out_specs=(far,) * 4,
         scratch_shapes=[pltpu.SemaphoreType.DMA((4,))],
+        compiler_params=pltpu.CompilerParams(vmem_limit_bytes=4 * 1024 * 1024),
     )(*results)
     return (
         vertex_out,

time: 65.2 us -> 66.6 us (1.021)
  Pallas kernels: 61.8 us -> 65.8 us
  local copies, waits for them, and re-layouts: 2.58 us -> 0 us
    pallas_call x1, Pallas kernels: 58.9 us -> 64.4 us  [body(): pl.pallas_call(functools.partial(kernel, n_outer, n_inner), out_shape=tup...]
    unnamed x8 -> x0, local copies, waits for them, and re-layouts: 2.58 us -> none
    pallas_call x1, Pallas kernels: 2.9 us -> 1.36 us  [body(): pl.pallas_call(store_kernel, out_shape=tuple((jax.ShapeDtypeStruct(shape,...]
where the time goes in v3:
time: 66.6 us; the launch traced here: 66.4 us
  Pallas kernels  65.8 us (99%)
    pallas_call x1, Pallas kernels, body(): pl.pallas_call(functools.partial(kernel, n_outer, n_inner), out_shape=tup...  64.4 us
    pallas_call x1, Pallas kernels, body(): pl.pallas_call(store_kernel, out_shape=tuple((jax.ShapeDtypeStruct(shape,...  1.36 us

profile of v3, /device:TPU:0, one launch (start us, length us, event | category | flops | bytes accessed | tf_op | source)
XLA Modules:
  0.0 66.4 jit_solution(13568778535375062231)
XLA Ops:
  0.6 64.4 %shard_map.93 = (f32[256,1024]{1,0:T(8,128)S(1)}, f32[1,256]{1,0:T(1,128)S(1)}, f32[16,16,1024]{2,1,0:T(8,128)S(1)}, f32[1,256]{1,0:T(1,128)S(1)}) custom-call(f32[256,1024]{1,0:T(8,128)} %vertex.1, f32[1,256]{1,0:T(1,128)} %bitcast.8, f32[16,16,1024]{2,1,0:T(8,128)} %bitcast.6, f32[1,256]{1,0:T(1,128)} %bitcast.9, s32[1,1536]{1,0:T(1,128)} %edge_source_in.1, ...), custom_call_target="tpu_custom_call" | custom-call | flops 1409286144 | bytes 4194304 | tf_op jit(solution)/shard_map/pallas_call | solution.py:261
  65.1 1.4 %shard_map.94 = (f32[256,1024]{1,0:T(8,128)}, f32[1,256]{1,0:T(1,128)}, f32[16,16,1024]{2,1,0:T(8,128)}, f32[1,256]{1,0:T(1,128)}) custom-call(f32[256,1024]{1,0:T(8,128)S(1)} %get-tuple-element.12.refs_0_, f32[1,256]{1,0:T(1,128)S(1)} %get-tuple-element.13.refs_1_, f32[16,16,1024]{2,1,0:T(8,128)S(1)} %get-tuple-element.14.refs_2_, ...), custom_call_target="tpu_custom_call" | custom-call | tf_op jit(solution)/shard_map/pallas_call | solution.py:300

commit v4 on v2

--- a/solution.py
+++ b/solution.py
@@ -95,13 +95,13 @@
             device_id_type=MESH,
         )
 
-    def state_hop(s):
+    def state_move(r):
         return pltpu.make_async_remote_copy(
-            src_ref=state.at[s],
-            dst_ref=state.at[s + pieces],
-            send_sem=state_send_sem.at[s],
-            recv_sem=state_recv_sem.at[s + pieces],
-            device_id=right,
+            src_ref=state.at[r],
+            dst_ref=state.at[r + 1],
+            send_sem=state_send_sem.at[r],
+            recv_sem=state_recv_sem.at[r],
+            device_id=ahead if r == ROUNDS - 1 else right,
             device_id_type=MESH,
         )
 
@@ -111,16 +111,6 @@
             dst_ref=context_out.at[k],
             send_sem=send_sem.at[hops + k],
             recv_sem=recv_sem.at[hops + pieces + k],
-            device_id=ahead,
-            device_id_type=MESH,
-        )
-
-    def state_leave(k):
-        return pltpu.make_async_remote_copy(
-            src_ref=state.at[hops + k],
-            dst_ref=state.at[hops + pieces + k],
-            send_sem=state_send_sem.at[hops + k],
-            recv_sem=state_recv_sem.at[hops + pieces + k],
             device_id=ahead,
             device_id_type=MESH,
         )
@@ -151,10 +141,10 @@
         place = lax.broadcasted_iota(jnp.int32, (chunk, block_rows), 0) + k * chunk
         lane = lax.broadcasted_iota(jnp.int32, (chunk, block_rows), 1)
         mine = place == lane
-        total = jnp.sum(jnp.where(mine, state[slot], 0.0), axis=1, keepdims=True)
-        total = total + jnp.sum(chunk_grad * chunk_grad, axis=1, keepdims=True) * (1.0 / width)
+        added = jnp.sum(chunk_grad * chunk_grad, axis=1, keepdims=True) * (1.0 / width)
+        total = jnp.sum(jnp.where(mine, state[r], 0.0), axis=1, keepdims=True) + added
         block[slot] = held - chunk_grad * (0.1 * lax.rsqrt(total))
-        state[slot] = jnp.sum(jnp.where(mine, total, 0.0), axis=0, keepdims=True)
+        state[r] += jnp.sum(jnp.where(mine, added, 0.0), axis=0, keepdims=True)
 
     def update_rows():
         rows_grad = lax.dot_general(
@@ -176,8 +166,7 @@
         jnp.int32, (row_count, row_count), 1
     )
     row_state[...] = jnp.sum(jnp.where(eye, vertex_state[...], 0.0), axis=1, keepdims=True)
-    for k in range(pieces):
-        state[k] = context_state[...]
+    state[0] = context_state[...]
     count(0)
     load_rows.wait()
     rows_b[...] = rows[...].astype(BF16)
@@ -185,7 +174,6 @@
     update_chunk(0, 0, 0)
     pl.semaphore_wait(barrier, 4)
     hop(0).start()
-    state_hop(0).start()
     load_rest.wait()
 
     @pl.loop(1, pieces)
@@ -195,8 +183,8 @@
         @pl.when(k < DEPTH)
         def _():
             hop(k).start()
-            state_hop(k).start()
-
+
+    state_move(0).start()
     for r in range(1, ROUNDS):
         count(r)
     update_rows()
@@ -207,20 +195,22 @@
         def _(k):
             s = (r - 1) * pieces + k
             hop(s).wait_send()
-            state_hop(s).wait_send()
 
             @pl.when(s + DEPTH < hops)
             def _():
                 hop(s + DEPTH).start()
-                state_hop(s + DEPTH).start()
 
             hop(s).wait_recv()
-            state_hop(s).wait_recv()
+
+            @pl.when(k == 0)
+            def _():
+                state_move(r - 1).wait_recv()
+
             update_chunk(s + pieces, r, k)
             if r == ROUNDS - 1:
                 leave(k).start()
-                state_leave(k).start()
-
+
+        state_move(r).start()
         update_rows()
 
     vertex_state_out[...] = jnp.sum(jnp.where(eye, row_state[...], 0.0), axis=0, keepdims=True)
@@ -228,9 +218,11 @@
     @pl.loop(0, pieces)
     def _(k):
         leave(k).wait()
-        state_leave(k).wait()
-
-    context_state_out[...] = jnp.sum(state[pl.ds(hops + pieces, pieces)], axis=0)
+
+    for r in range(ROUNDS):
+        state_move(r).wait_send()
+    state_move(ROUNDS - 1).wait_recv()
+    context_state_out[...] = state[ROUNDS]
 
 
 def store_kernel(*refs):
@@ -271,15 +263,15 @@
             pltpu.VMEM((row_count, width), BF16),
             pltpu.VMEM((row_count, 1), F32),
             pltpu.VMEM((slots, CHUNK, width), F32),
-            pltpu.VMEM((slots + pieces, 1, block_rows), F32),
+            pltpu.VMEM((ROUNDS + 1, 1, block_rows), F32),
             pltpu.VMEM((pieces, CHUNK, width), BF16),
             pltpu.VMEM((pieces, CHUNK, row_count), BF16),
             pltpu.VMEM((ROUNDS, pieces, CHUNK, row_count), F32),
             pltpu.SemaphoreType.DMA((7,)),
             pltpu.SemaphoreType.DMA((slots,)),
             pltpu.SemaphoreType.DMA((slots + pieces,)),
-            pltpu.SemaphoreType.DMA((slots,)),
-            pltpu.SemaphoreType.DMA((slots + pieces,)),
+            pltpu.SemaphoreType.DMA((ROUNDS,)),
+            pltpu.SemaphoreType.DMA((ROUNDS,)),
         ],
         compiler_params=pltpu.CompilerParams(
             collective_id=0, has_side_effects=True, vmem_limit_bytes=56 * 1024 * 1024
@@ -303,6 +295,7 @@
         in_specs=[near] * 4,
         out_specs=(far,) * 4,
         scratch_shapes=[pltpu.SemaphoreType.DMA((4,))],
+        compiler_params=pltpu.CompilerParams(vmem_limit_bytes=4 * 1024 * 1024),
     )(*results)
     return (
         vertex_out,

time: 65.2 us -> 59.8 us (0.917)
  Pallas kernels: 61.8 us -> 58.9 us
  local copies, waits for them, and re-layouts: 2.58 us -> 0 us
    unnamed x8 -> x0, local copies, waits for them, and re-layouts: 2.58 us -> none
    pallas_call x1, Pallas kernels: 2.9 us -> 1.36 us  [body(): pl.pallas_call(store_kernel, out_shape=tuple((jax.ShapeDtypeStruct(shape,...]
    pallas_call x1, Pallas kernels: 58.9 us -> 57.6 us  [body(): pl.pallas_call(functools.partial(kernel, n_outer, n_inner), out_shape=tup...]
where the time goes in v4:
time: 59.8 us; the launch traced here: 59.6 us
  Pallas kernels  58.9 us (98%)
  between operations  0.64 us (1%)
    pallas_call x1, Pallas kernels, body(): pl.pallas_call(functools.partial(kernel, n_outer, n_inner), out_shape=tup...  57.6 us
    pallas_call x1, Pallas kernels, body(): pl.pallas_call(store_kernel, out_shape=tuple((jax.ShapeDtypeStruct(shape,...  1.36 us

profile of v4, /device:TPU:0, one launch (start us, length us, event | category | flops | bytes accessed | tf_op | source)
XLA Modules:
  0.0 59.6 jit_solution(1905817075291800825)
XLA Ops:
  0.6 57.6 %shard_map.93 = (f32[256,1024]{1,0:T(8,128)S(1)}, f32[1,256]{1,0:T(1,128)S(1)}, f32[8,32,1024]{2,1,0:T(8,128)S(1)}, f32[1,256]{1,0:T(1,128)S(1)}) custom-call(f32[256,1024]{1,0:T(8,128)} %vertex.1, f32[1,256]{1,0:T(1,128)} %bitcast.8, f32[8,32,1024]{2,1,0:T(8,128)} %bitcast.6, f32[1,256]{1,0:T(1,128)} %bitcast.9, s32[1,1536]{1,0:T(1,128)} %edge_source_in.1, ...), custom_call_target="tpu_custom_call" | custom-call | flops 1409286144 | bytes 4194304 | tf_op jit(solution)/shard_map/pallas_call | solution.py:253
  58.2 1.4 %shard_map.94 = (f32[256,1024]{1,0:T(8,128)}, f32[1,256]{1,0:T(1,128)}, f32[8,32,1024]{2,1,0:T(8,128)}, f32[1,256]{1,0:T(1,128)}) custom-call(f32[256,1024]{1,0:T(8,128)S(1)} %get-tuple-element.12.refs_0_, f32[1,256]{1,0:T(1,128)S(1)} %get-tuple-element.13.refs_1_, f32[8,32,1024]{2,1,0:T(8,128)S(1)} %get-tuple-element.14.refs_2_, ...), custom_call_target="tpu_custom_call" | custom-call | tf_op jit(solution)/shard_map/pallas_call | solution.py:292

commit v5 on v4

--- a/solution.py
+++ b/solution.py
@@ -34,6 +34,7 @@
     edge_source,
     edge_target,
     rows_b,
+    rows_t,
     row_state,
     block,
     state,
@@ -76,12 +77,17 @@
     ]
     for load in small_loads:
         load.start()
-    load_rows = pltpu.make_async_copy(vertex, rows, load_sem.at[0])
+    halves = [pl.ds(0, row_count // 2), pl.ds(row_count // 2, row_count // 2)]
+    load_rows = [
+        pltpu.make_async_copy(vertex.at[half], rows.at[half], load_sem.at[7 * n])
+        for n, half in enumerate(halves)
+    ]
     load_first = pltpu.make_async_copy(context.at[0], block.at[0], load_sem.at[1])
     load_rest = pltpu.make_async_copy(
         context.at[pl.ds(1, pieces - 1)], block.at[pl.ds(1, pieces - 1)], load_sem.at[2]
     )
-    load_rows.start()
+    for load in load_rows:
+        load.start()
     load_first.start()
     load_rest.start()
 
@@ -132,7 +138,7 @@
         held_b = held.astype(BF16)
         block_b[k] = held_b
         scores = lax.dot_general(
-            held_b, rows_b[...], (((1,), (1,)), ((), ())), preferred_element_type=F32
+            held_b, rows_t[...], (((1,), (0,)), ((), ())), preferred_element_type=F32
         )
         prob = 1.0 / (1.0 + jnp.exp(-scores))
         grad = (prob * (1.0 / block_rows) - counts[r, k] * (1.0 - prob)).astype(BF16)
@@ -146,7 +152,12 @@
         block[slot] = held - chunk_grad * (0.1 * lax.rsqrt(total))
         state[r] += jnp.sum(jnp.where(mine, added, 0.0), axis=0, keepdims=True)
 
-    def update_rows():
+    def round_rows():
+        rounded = rows[...].astype(BF16)
+        rows_b[...] = rounded
+        rows_t[...] = rounded.T
+
+    def update_rows(last):
         rows_grad = lax.dot_general(
             grads[...].reshape(block_rows, row_count),
             block_b[...].reshape(block_rows, width),
@@ -158,22 +169,24 @@
         )
         row_state[...] = total
         rows[...] = rows[...] - rows_grad * (0.1 * lax.rsqrt(total))
-        rows_b[...] = rows[...].astype(BF16)
+        if not last:
+            round_rows()
 
     for load in small_loads:
         load.wait()
-    eye = lax.broadcasted_iota(jnp.int32, (row_count, row_count), 0) == lax.broadcasted_iota(
-        jnp.int32, (row_count, row_count), 1
-    )
-    row_state[...] = jnp.sum(jnp.where(eye, vertex_state[...], 0.0), axis=1, keepdims=True)
     state[0] = context_state[...]
     count(0)
-    load_rows.wait()
-    rows_b[...] = rows[...].astype(BF16)
+    for load in load_rows:
+        load.wait()
+    round_rows()
     load_first.wait()
     update_chunk(0, 0, 0)
     pl.semaphore_wait(barrier, 4)
     hop(0).start()
+    eye = lax.broadcasted_iota(jnp.int32, (row_count, row_count), 0) == lax.broadcasted_iota(
+        jnp.int32, (row_count, row_count), 1
+    )
+    row_state[...] = jnp.sum(jnp.where(eye, vertex_state[...], 0.0), axis=1, keepdims=True)
     load_rest.wait()
 
     @pl.loop(1, pieces)
@@ -187,7 +200,7 @@
     state_move(0).start()
     for r in range(1, ROUNDS):
         count(r)
-    update_rows()
+    update_rows(False)
 
     for r in range(1, ROUNDS):
 
@@ -211,7 +224,7 @@
                 leave(k).start()
 
         state_move(r).start()
-        update_rows()
+        update_rows(r == ROUNDS - 1)
 
     vertex_state_out[...] = jnp.sum(jnp.where(eye, row_state[...], 0.0), axis=0, keepdims=True)
 
@@ -227,9 +240,16 @@
 
 def store_kernel(*refs):
     sources, targets, sems = refs[:4], refs[4:8], refs[8]
+    pairs = []
+    for source, target in zip(sources, targets):
+        lead = source.shape[0]
+        parts = 1 if lead == 1 else 2
+        for part in range(parts):
+            span = pl.ds(part * (lead // parts), lead // parts)
+            pairs.append((source.at[span], target.at[span]))
     copies = [
         pltpu.make_async_copy(source, target, sems.at[n])
-        for n, (source, target) in enumerate(zip(sources, targets))
+        for n, (source, target) in enumerate(pairs)
     ]
     for copy in copies:
         copy.start()
@@ -261,13 +281,14 @@
             pltpu.VMEM(edge_source.shape, jnp.int32),
             pltpu.VMEM(edge_target.shape, jnp.int32),
             pltpu.VMEM((row_count, width), BF16),
+            pltpu.VMEM((width, row_count), BF16),
             pltpu.VMEM((row_count, 1), F32),
             pltpu.VMEM((slots, CHUNK, width), F32),
             pltpu.VMEM((ROUNDS + 1, 1, block_rows), F32),
             pltpu.VMEM((pieces, CHUNK, width), BF16),
             pltpu.VMEM((pieces, CHUNK, row_count), BF16),
             pltpu.VMEM((ROUNDS, pieces, CHUNK, row_count), F32),
-            pltpu.SemaphoreType.DMA((7,)),
+            pltpu.SemaphoreType.DMA((8,)),
             pltpu.SemaphoreType.DMA((slots,)),
             pltpu.SemaphoreType.DMA((slots + pieces,)),
             pltpu.SemaphoreType.DMA((ROUNDS,)),
@@ -294,7 +315,7 @@
         out_shape=tuple(jax.ShapeDtypeStruct(shape, F32) for shape in shapes),
         in_specs=[near] * 4,
         out_specs=(far,) * 4,
-        scratch_shapes=[pltpu.SemaphoreType.DMA((4,))],
+        scratch_shapes=[pltpu.SemaphoreType.DMA((6,))],
         compiler_params=pltpu.CompilerParams(vmem_limit_bytes=4 * 1024 * 1024),
     )(*results)
     return (

time: 59.8 us -> 59.8 us (level)
  no operation moved by 1% of the time
where the time goes in v5:
time: 59.8 us; the launch traced here: 59.6 us
  Pallas kernels  58.9 us (98%)
  between operations  0.64 us (1%)
    pallas_call x1, Pallas kernels, body(): pl.pallas_call(functools.partial(kernel, n_outer, n_inner), out_shape=tup...  57.6 us
    pallas_call x1, Pallas kernels, body(): pl.pallas_call(store_kernel, out_shape=tuple((jax.ShapeDtypeStruct(shape,...  1.37 us

profile of v5, /device:TPU:0, one launch (start us, length us, event | category | flops | bytes accessed | tf_op | source)
XLA Modules:
  0.0 59.6 jit_solution(10799440403911257263)
XLA Ops:
  0.6 57.6 %shard_map.93 = (f32[256,1024]{1,0:T(8,128)S(1)}, f32[1,256]{1,0:T(1,128)S(1)}, f32[8,32,1024]{2,1,0:T(8,128)S(1)}, f32[1,256]{1,0:T(1,128)S(1)}) custom-call(f32[256,1024]{1,0:T(8,128)} %vertex.1, f32[1,256]{1,0:T(1,128)} %bitcast.8, f32[8,32,1024]{2,1,0:T(8,128)} %bitcast.6, f32[1,256]{1,0:T(1,128)} %bitcast.9, s32[1,1536]{1,0:T(1,128)} %edge_source_in.1, ...), custom_call_target="tpu_custom_call" | custom-call | flops 1409286144 | bytes 4194304 | tf_op jit(solution)/shard_map/pallas_call | solution.py:273
  58.2 1.4 %shard_map.94 = (f32[256,1024]{1,0:T(8,128)}, f32[1,256]{1,0:T(1,128)}, f32[8,32,1024]{2,1,0:T(8,128)}, f32[1,256]{1,0:T(1,128)}) custom-call(f32[256,1024]{1,0:T(8,128)S(1)} %get-tuple-element.12.refs_0_, f32[1,256]{1,0:T(1,128)S(1)} %get-tuple-element.13.refs_1_, f32[8,32,1024]{2,1,0:T(8,128)S(1)} %get-tuple-element.14.refs_2_, ...), custom_call_target="tpu_custom_call" | custom-call | tf_op jit(solution)/shard_map/pallas_call | solution.py:313

commit v6 on v5

--- a/solution.py
+++ b/solution.py
@@ -9,7 +9,7 @@
 
 ROUNDS = 3
 CHUNK = 32
-DEPTH = 4
+DEPTH = 2
 
 MESH = pl.DeviceIdType.MESH
 BF16 = jnp.bfloat16

time: 59.8 us -> 60 us (level)
  no operation moved by 1% of the time
where the time goes in v6:
time: 60 us; the launch traced here: 59.7 us
  Pallas kernels  59.1 us (98%)
  between operations  0.64 us (1%)
    pallas_call x1, Pallas kernels, body(): pl.pallas_call(functools.partial(kernel, n_outer, n_inner), out_shape=tup...  57.7 us
    pallas_call x1, Pallas kernels, body(): pl.pallas_call(store_kernel, out_shape=tuple((jax.ShapeDtypeStruct(shape,...  1.37 us

profile of v6, /device:TPU:0, one launch (start us, length us, event | category | flops | bytes accessed | tf_op | source)
XLA Modules:
  0.0 59.7 jit_solution(8007506075723567525)
XLA Ops:
  0.6 57.7 %shard_map.93 = (f32[256,1024]{1,0:T(8,128)S(1)}, f32[1,256]{1,0:T(1,128)S(1)}, f32[8,32,1024]{2,1,0:T(8,128)S(1)}, f32[1,256]{1,0:T(1,128)S(1)}) custom-call(f32[256,1024]{1,0:T(8,128)} %vertex.1, f32[1,256]{1,0:T(1,128)} %bitcast.8, f32[8,32,1024]{2,1,0:T(8,128)} %bitcast.6, f32[1,256]{1,0:T(1,128)} %bitcast.9, s32[1,1536]{1,0:T(1,128)} %edge_source_in.1, ...), custom_call_target="tpu_custom_call" | custom-call | flops 1409286144 | bytes 4194304 | tf_op jit(solution)/shard_map/pallas_call | solution.py:273
  58.4 1.4 %shard_map.94 = (f32[256,1024]{1,0:T(8,128)}, f32[1,256]{1,0:T(1,128)}, f32[8,32,1024]{2,1,0:T(8,128)}, f32[1,256]{1,0:T(1,128)}) custom-call(f32[256,1024]{1,0:T(8,128)S(1)} %get-tuple-element.12.refs_0_, f32[1,256]{1,0:T(1,128)S(1)} %get-tuple-element.13.refs_1_, f32[8,32,1024]{2,1,0:T(8,128)S(1)} %get-tuple-element.14.refs_2_, ...), custom_call_target="tpu_custom_call" | custom-call | tf_op jit(solution)/shard_map/pallas_call | solution.py:313

commit v7 on v5

--- a/solution.py
+++ b/solution.py
@@ -101,6 +101,28 @@
             device_id_type=MESH,
         )
 
+    def half_hop(h):
+        span = pl.ds(h * (chunk // 2), chunk // 2)
+        return pltpu.make_async_remote_copy(
+            src_ref=block.at[hops - 1, span],
+            dst_ref=block.at[hops - 1 + pieces, span],
+            send_sem=send_sem.at[hops - 1 if h == 0 else hops + pieces],
+            recv_sem=recv_sem.at[hops - 1 + pieces if h == 0 else hops + 2 * pieces],
+            device_id=right,
+            device_id_type=MESH,
+        )
+
+    def half_leave(h):
+        span = pl.ds(h * (chunk // 2), chunk // 2)
+        return pltpu.make_async_remote_copy(
+            src_ref=block.at[hops - 1 + pieces, span],
+            dst_ref=context_out.at[pieces - 1, span],
+            send_sem=send_sem.at[hops + pieces - 1 + 2 * h],
+            recv_sem=recv_sem.at[hops + 2 * pieces - 1 + 2 * h],
+            device_id=ahead,
+            device_id_type=MESH,
+        )
+
     def state_move(r):
         return pltpu.make_async_remote_copy(
             src_ref=state.at[r],
@@ -133,23 +155,24 @@
             target_hot, source_hot, (((1,), (1,)), ((), ())), preferred_element_type=F32
         ).reshape(pieces, chunk, row_count)
 
-    def update_chunk(slot, r, k):
-        held = block[slot]
+    def update_chunk(slot, r, k, at=0, size=chunk):
+        span = pl.ds(at, size)
+        held = block[slot, span]
         held_b = held.astype(BF16)
-        block_b[k] = held_b
+        block_b[k, span] = held_b
         scores = lax.dot_general(
             held_b, rows_t[...], (((1,), (0,)), ((), ())), preferred_element_type=F32
         )
         prob = 1.0 / (1.0 + jnp.exp(-scores))
-        grad = (prob * (1.0 / block_rows) - counts[r, k] * (1.0 - prob)).astype(BF16)
-        grads[k] = grad
+        grad = (prob * (1.0 / block_rows) - counts[r, k, span] * (1.0 - prob)).astype(BF16)
+        grads[k, span] = grad
         chunk_grad = jnp.dot(grad, rows_b[...], preferred_element_type=F32)
-        place = lax.broadcasted_iota(jnp.int32, (chunk, block_rows), 0) + k * chunk
-        lane = lax.broadcasted_iota(jnp.int32, (chunk, block_rows), 1)
+        place = lax.broadcasted_iota(jnp.int32, (size, block_rows), 0) + (k * chunk + at)
+        lane = lax.broadcasted_iota(jnp.int32, (size, block_rows), 1)
         mine = place == lane
         added = jnp.sum(chunk_grad * chunk_grad, axis=1, keepdims=True) * (1.0 / width)
         total = jnp.sum(jnp.where(mine, state[r], 0.0), axis=1, keepdims=True) + added
-        block[slot] = held - chunk_grad * (0.1 * lax.rsqrt(total))
+        block[slot, span] = held - chunk_grad * (0.1 * lax.rsqrt(total))
         state[r] += jnp.sum(jnp.where(mine, added, 0.0), axis=0, keepdims=True)
 
     def round_rows():
@@ -204,14 +227,21 @@
 
     for r in range(1, ROUNDS):
 
-        @pl.loop(0, pieces)
+        last = r == ROUNDS - 1
+
+        @pl.loop(0, pieces - 1 if last else pieces)
         def _(k):
             s = (r - 1) * pieces + k
             hop(s).wait_send()
 
-            @pl.when(s + DEPTH < hops)
+            @pl.when(s + DEPTH < hops - 1)
             def _():
                 hop(s + DEPTH).start()
+
+            @pl.when(s + DEPTH == hops - 1)
+            def _():
+                half_hop(0).start()
+                half_hop(1).start()
 
             hop(s).wait_recv()
 
@@ -220,17 +250,25 @@
                 state_move(r - 1).wait_recv()
 
             update_chunk(s + pieces, r, k)
-            if r == ROUNDS - 1:
+            if last:
                 leave(k).start()
 
+        if last:
+            for h in range(2):
+                half_hop(h).wait()
+                update_chunk(hops - 1 + pieces, r, pieces - 1, h * (chunk // 2), chunk // 2)
+                half_leave(h).start()
         state_move(r).start()
-        update_rows(r == ROUNDS - 1)
+        update_rows(last)
 
     vertex_state_out[...] = jnp.sum(jnp.where(eye, row_state[...], 0.0), axis=0, keepdims=True)
 
-    @pl.loop(0, pieces)
+    @pl.loop(0, pieces - 1)
     def _(k):
         leave(k).wait()
+
+    for h in range(2):
+        half_leave(h).wait()
 
     for r in range(ROUNDS):
         state_move(r).wait_send()
@@ -289,8 +327,8 @@
             pltpu.VMEM((pieces, CHUNK, row_count), BF16),
             pltpu.VMEM((ROUNDS, pieces, CHUNK, row_count), F32),
             pltpu.SemaphoreType.DMA((8,)),
-            pltpu.SemaphoreType.DMA((slots,)),
-            pltpu.SemaphoreType.DMA((slots + pieces,)),
+            pltpu.SemaphoreType.DMA((slots + 2,)),
+            pltpu.SemaphoreType.DMA((slots + pieces + 2,)),
             pltpu.SemaphoreType.DMA((ROUNDS,)),
             pltpu.SemaphoreType.DMA((ROUNDS,)),
         ],

time: 59.8 us -> 59.1 us (0.988)
  Pallas kernels: 58.9 us -> 58.3 us
    pallas_call x1, Pallas kernels: 57.6 us -> 56.9 us  [body(): pl.pallas_call(functools.partial(kernel, n_outer, n_inner), out_shape=tup...]
where the time goes in v7:
time: 59.1 us; the launch traced here: 58.9 us
  Pallas kernels  58.3 us (99%)
  between operations  0.64 us (1%)
    pallas_call x1, Pallas kernels, body(): pl.pallas_call(functools.partial(kernel, n_outer, n_inner), out_shape=tup...  56.9 us
    pallas_call x1, Pallas kernels, body(): pl.pallas_call(store_kernel, out_shape=tuple((jax.ShapeDtypeStruct(shape,...  1.37 us

profile of v7, /device:TPU:0, one launch (start us, length us, event | category | flops | bytes accessed | tf_op | source)
XLA Modules:
  0.0 58.9 jit_solution(6452224897770156007)
XLA Ops:
  0.6 56.9 %shard_map.93 = (f32[256,1024]{1,0:T(8,128)S(1)}, f32[1,256]{1,0:T(1,128)S(1)}, f32[8,32,1024]{2,1,0:T(8,128)S(1)}, f32[1,256]{1,0:T(1,128)S(1)}) custom-call(f32[256,1024]{1,0:T(8,128)} %vertex.1, f32[1,256]{1,0:T(1,128)} %bitcast.8, f32[8,32,1024]{2,1,0:T(8,128)} %bitcast.6, f32[1,256]{1,0:T(1,128)} %bitcast.9, s32[1,1536]{1,0:T(1,128)} %edge_source_in.1, ...), custom_call_target="tpu_custom_call" | custom-call | flops 1409286144 | bytes 4194304 | tf_op jit(solution)/shard_map/pallas_call | solution.py:311
  57.5 1.4 %shard_map.94 = (f32[256,1024]{1,0:T(8,128)}, f32[1,256]{1,0:T(1,128)}, f32[8,32,1024]{2,1,0:T(8,128)}, f32[1,256]{1,0:T(1,128)}) custom-call(f32[256,1024]{1,0:T(8,128)S(1)} %get-tuple-element.12.refs_0_, f32[1,256]{1,0:T(1,128)S(1)} %get-tuple-element.13.refs_1_, f32[8,32,1024]{2,1,0:T(8,128)S(1)} %get-tuple-element.14.refs_2_, ...), custom_call_target="tpu_custom_call" | custom-call | tf_op jit(solution)/shard_map/pallas_call | solution.py:351

commit v8 on v7

--- a/solution.py
+++ b/solution.py
@@ -60,10 +60,6 @@
     ahead = {"outer": lax.rem(o + 1, n_outer)}
     behind = {"outer": lax.rem(o + n_outer - 1, n_outer)}
 
-    barrier = pltpu.get_barrier_semaphore()
-    for neighbour in (left, right, behind, ahead):
-        pl.semaphore_signal(barrier, inc=1, device_id=neighbour, device_id_type=MESH)
-
     small_loads = [
         pltpu.make_async_copy(source, target, load_sem.at[3 + n])
         for n, (source, target) in enumerate(
@@ -91,6 +87,10 @@
     load_first.start()
     load_rest.start()
 
+    barrier = pltpu.get_barrier_semaphore()
+    for neighbour in (left, right, behind, ahead):
+        pl.semaphore_signal(barrier, inc=1, device_id=neighbour, device_id_type=MESH)
+
     def hop(s):
         return pltpu.make_async_remote_copy(
             src_ref=block.at[s],
@@ -143,17 +143,18 @@
             device_id_type=MESH,
         )
 
-    def count(r):
+    def count(r, first, number):
         span = pl.ds(r * edges, edges)
         target_hot = (
-            edge_target[:, span] == lax.broadcasted_iota(jnp.int32, (block_rows, edges), 0)
+            edge_target[:, span]
+            == lax.broadcasted_iota(jnp.int32, (number * chunk, edges), 0) + first * chunk
         ).astype(F32).astype(BF16)
         source_hot = (
             edge_source[:, span] == lax.broadcasted_iota(jnp.int32, (row_count, edges), 0)
         ).astype(F32).astype(BF16)
-        counts[r] = lax.dot_general(
+        counts[r, pl.ds(first, number)] = lax.dot_general(
             target_hot, source_hot, (((1,), (1,)), ((), ())), preferred_element_type=F32
-        ).reshape(pieces, chunk, row_count)
+        ).reshape(number, chunk, row_count)
 
     def update_chunk(slot, r, k, at=0, size=chunk):
         span = pl.ds(at, size)
@@ -175,10 +176,10 @@
         block[slot, span] = held - chunk_grad * (0.1 * lax.rsqrt(total))
         state[r] += jnp.sum(jnp.where(mine, added, 0.0), axis=0, keepdims=True)
 
-    def round_rows():
-        rounded = rows[...].astype(BF16)
-        rows_b[...] = rounded
-        rows_t[...] = rounded.T
+    def round_rows(half):
+        rounded = rows[half].astype(BF16)
+        rows_b[half] = rounded
+        rows_t[:, half] = rounded.T
 
     def update_rows(last):
         rows_grad = lax.dot_general(
@@ -193,19 +194,21 @@
         row_state[...] = total
         rows[...] = rows[...] - rows_grad * (0.1 * lax.rsqrt(total))
         if not last:
-            round_rows()
+            for half in halves:
+                round_rows(half)
 
     for load in small_loads:
         load.wait()
     state[0] = context_state[...]
-    count(0)
-    for load in load_rows:
+    count(0, 0, 1)
+    for half, load in zip(halves, load_rows):
         load.wait()
-    round_rows()
+        round_rows(half)
     load_first.wait()
     update_chunk(0, 0, 0)
     pl.semaphore_wait(barrier, 4)
     hop(0).start()
+    count(0, 1, pieces - 1)
     eye = lax.broadcasted_iota(jnp.int32, (row_count, row_count), 0) == lax.broadcasted_iota(
         jnp.int32, (row_count, row_count), 1
     )
@@ -222,7 +225,7 @@
 
     state_move(0).start()
     for r in range(1, ROUNDS):
-        count(r)
+        count(r, 0, pieces)
     update_rows(False)
 
     for r in range(1, ROUNDS):

time: 59.1 us -> 59 us (level)
  no operation moved by 1% of the time
where the time goes in v8:
time: 59 us; the launch traced here: 58.8 us
  Pallas kernels  58.1 us (98%)
  between operations  0.64 us (1%)
    pallas_call x1, Pallas kernels, body(): pl.pallas_call(functools.partial(kernel, n_outer, n_inner), out_shape=tup...  56.8 us
    pallas_call x1, Pallas kernels, body(): pl.pallas_call(store_kernel, out_shape=tuple((jax.ShapeDtypeStruct(shape,...  1.37 us

profile of v8, /device:TPU:0, one launch (start us, length us, event | category | flops | bytes accessed | tf_op | source)
XLA Modules:
  0.0 58.8 jit_solution(9215101274510827422)
XLA Ops:
  0.6 56.8 %shard_map.93 = (f32[256,1024]{1,0:T(8,128)S(1)}, f32[1,256]{1,0:T(1,128)S(1)}, f32[8,32,1024]{2,1,0:T(8,128)S(1)}, f32[1,256]{1,0:T(1,128)S(1)}) custom-call(f32[256,1024]{1,0:T(8,128)} %vertex.1, f32[1,256]{1,0:T(1,128)} %bitcast.8, f32[8,32,1024]{2,1,0:T(8,128)} %bitcast.6, f32[1,256]{1,0:T(1,128)} %bitcast.9, s32[1,1536]{1,0:T(1,128)} %edge_source_in.1, ...), custom_call_target="tpu_custom_call" | custom-call | flops 1409286144 | bytes 4194304 | tf_op jit(solution)/shard_map/pallas_call | solution.py:314
  57.4 1.4 %shard_map.94 = (f32[256,1024]{1,0:T(8,128)}, f32[1,256]{1,0:T(1,128)}, f32[8,32,1024]{2,1,0:T(8,128)}, f32[1,256]{1,0:T(1,128)}) custom-call(f32[256,1024]{1,0:T(8,128)S(1)} %get-tuple-element.12.refs_0_, f32[1,256]{1,0:T(1,128)S(1)} %get-tuple-element.13.refs_1_, f32[8,32,1024]{2,1,0:T(8,128)S(1)} %get-tuple-element.14.refs_2_, ...), custom_call_target="tpu_custom_call" | custom-call | tf_op jit(solution)/shard_map/pallas_call | solution.py:354

commit v9 on v8

--- a/solution.py
+++ b/solution.py
@@ -8,8 +8,8 @@
 from jax.sharding import PartitionSpec as P
 
 ROUNDS = 3
-CHUNK = 32
-DEPTH = 4
+CHUNK = 64
+DEPTH = 2
 
 MESH = pl.DeviceIdType.MESH
 BF16 = jnp.bfloat16
@@ -52,6 +52,8 @@
     block_rows = pieces * chunk
     edges = edge_source_in.shape[1] // ROUNDS
     hops = (ROUNDS - 1) * pieces
+    slots = ROUNDS * pieces
+    parts = ((0, chunk // 2), (chunk // 2, chunk // 4), (3 * chunk // 4, chunk // 4))
 
     i = lax.axis_index("inner")
     o = lax.axis_index("outer")
@@ -88,7 +90,7 @@
     load_rest.start()
 
     barrier = pltpu.get_barrier_semaphore()
-    for neighbour in (left, right, behind, ahead):
+    for neighbour in (left, behind):
         pl.semaphore_signal(barrier, inc=1, device_id=neighbour, device_id_type=MESH)
 
     def hop(s):
@@ -101,24 +103,24 @@
             device_id_type=MESH,
         )
 
-    def half_hop(h):
-        span = pl.ds(h * (chunk // 2), chunk // 2)
+    def part_hop(h):
+        span = pl.ds(*parts[h])
         return pltpu.make_async_remote_copy(
             src_ref=block.at[hops - 1, span],
             dst_ref=block.at[hops - 1 + pieces, span],
-            send_sem=send_sem.at[hops - 1 if h == 0 else hops + pieces],
-            recv_sem=recv_sem.at[hops - 1 + pieces if h == 0 else hops + 2 * pieces],
+            send_sem=send_sem.at[hops - 1 if h == 0 else slots + h - 1],
+            recv_sem=recv_sem.at[slots - 1 if h == 0 else slots + pieces + h - 1],
             device_id=right,
             device_id_type=MESH,
         )
 
-    def half_leave(h):
-        span = pl.ds(h * (chunk // 2), chunk // 2)
+    def part_leave(h):
+        span = pl.ds(*parts[h])
         return pltpu.make_async_remote_copy(
             src_ref=block.at[hops - 1 + pieces, span],
             dst_ref=context_out.at[pieces - 1, span],
-            send_sem=send_sem.at[hops + pieces - 1 + 2 * h],
-            recv_sem=recv_sem.at[hops + 2 * pieces - 1 + 2 * h],
+            send_sem=send_sem.at[slots - 1 if h == 0 else slots + h + 1],
+            recv_sem=recv_sem.at[slots + pieces - 1 if h == 0 else slots + pieces + h + 1],
             device_id=ahead,
             device_id_type=MESH,
         )
@@ -206,7 +208,7 @@
         round_rows(half)
     load_first.wait()
     update_chunk(0, 0, 0)
-    pl.semaphore_wait(barrier, 4)
+    pl.semaphore_wait(barrier, 2)
     hop(0).start()
     count(0, 1, pieces - 1)
     eye = lax.broadcasted_iota(jnp.int32, (row_count, row_count), 0) == lax.broadcasted_iota(
@@ -243,8 +245,8 @@
 
             @pl.when(s + DEPTH == hops - 1)
             def _():
-                half_hop(0).start()
-                half_hop(1).start()
+                for h in range(len(parts)):
+                    part_hop(h).start()
 
             hop(s).wait_recv()
 
@@ -257,10 +259,10 @@
                 leave(k).start()
 
         if last:
-            for h in range(2):
-                half_hop(h).wait()
-                update_chunk(hops - 1 + pieces, r, pieces - 1, h * (chunk // 2), chunk // 2)
-                half_leave(h).start()
+            for h in range(len(parts)):
+                part_hop(h).wait()
+                update_chunk(hops - 1 + pieces, r, pieces - 1, *parts[h])
+                part_leave(h).start()
         state_move(r).start()
         update_rows(last)
 
@@ -270,8 +272,8 @@
     def _(k):
         leave(k).wait()
 
-    for h in range(2):
-        half_leave(h).wait()
+    for h in range(len(parts)):
+        part_leave(h).wait()
 
     for r in range(ROUNDS):
         state_move(r).wait_send()
@@ -330,8 +332,8 @@
             pltpu.VMEM((pieces, CHUNK, row_count), BF16),
             pltpu.VMEM((ROUNDS, pieces, CHUNK, row_count), F32),
             pltpu.SemaphoreType.DMA((8,)),
-            pltpu.SemaphoreType.DMA((slots + 2,)),
-            pltpu.SemaphoreType.DMA((slots + pieces + 2,)),
+            pltpu.SemaphoreType.DMA((slots + 4,)),
+            pltpu.SemaphoreType.DMA((slots + pieces + 4,)),
             pltpu.SemaphoreType.DMA((ROUNDS,)),
             pltpu.SemaphoreType.DMA((ROUNDS,)),
         ],

time: 59 us -> 59.3 us (level)
  no operation moved by 1% of the time
where the time goes in v9:
time: 59.3 us; the launch traced here: 59.1 us
  Pallas kernels  58.4 us (98%)
  between operations  0.64 us (1%)
    pallas_call x1, Pallas kernels, body(): pl.pallas_call(functools.partial(kernel, n_outer, n_inner), out_shape=tup...  57.1 us
    pallas_call x1, Pallas kernels, body(): pl.pallas_call(store_kernel, out_shape=tuple((jax.ShapeDtypeStruct(shape,...  1.37 us

profile of v9, /device:TPU:0, one launch (start us, length us, event | category | flops | bytes accessed | tf_op | source)
XLA Modules:
  0.0 59.1 jit_solution(12742529809379637142)
XLA Ops:
  0.6 57.1 %shard_map.93 = (f32[256,1024]{1,0:T(8,128)S(1)}, f32[1,256]{1,0:T(1,128)S(1)}, f32[4,64,1024]{2,1,0:T(8,128)S(1)}, f32[1,256]{1,0:T(1,128)S(1)}) custom-call(f32[256,1024]{1,0:T(8,128)} %vertex.1, f32[1,256]{1,0:T(1,128)} %bitcast.8, f32[4,64,1024]{2,1,0:T(8,128)} %bitcast.6, f32[1,256]{1,0:T(1,128)} %bitcast.9, s32[1,1536]{1,0:T(1,128)} %edge_source_in.1, ...), custom_call_target="tpu_custom_call" | custom-call | flops 1409286144 | bytes 4194304 | tf_op jit(solution)/shard_map/pallas_call | solution.py:316
  57.7 1.4 %shard_map.94 = (f32[256,1024]{1,0:T(8,128)}, f32[1,256]{1,0:T(1,128)}, f32[4,64,1024]{2,1,0:T(8,128)}, f32[1,256]{1,0:T(1,128)}) custom-call(f32[256,1024]{1,0:T(8,128)S(1)} %get-tuple-element.12.refs_0_, f32[1,256]{1,0:T(1,128)S(1)} %get-tuple-element.13.refs_1_, f32[4,64,1024]{2,1,0:T(8,128)S(1)} %get-tuple-element.14.refs_2_, ...), custom_call_target="tpu_custom_call" | custom-call | tf_op jit(solution)/shard_map/pallas_call | solution.py:356

commit v10 on v8

--- a/solution.py
+++ b/solution.py
@@ -182,19 +182,19 @@
         rows_t[:, half] = rounded.T
 
     def update_rows(last):
-        rows_grad = lax.dot_general(
-            grads[...].reshape(block_rows, row_count),
-            block_b[...].reshape(block_rows, width),
-            (((0,), (0,)), ((), ())),
-            preferred_element_type=F32,
-        )
-        total = row_state[...] + jnp.sum(rows_grad * rows_grad, axis=1, keepdims=True) * (
-            1.0 / width
-        )
-        row_state[...] = total
-        rows[...] = rows[...] - rows_grad * (0.1 * lax.rsqrt(total))
-        if not last:
-            for half in halves:
+        for half in halves:
+            rows_grad = lax.dot_general(
+                grads[:, :, half].reshape(block_rows, row_count // 2),
+                block_b[...].reshape(block_rows, width),
+                (((0,), (0,)), ((), ())),
+                preferred_element_type=F32,
+            )
+            total = row_state[half] + jnp.sum(rows_grad * rows_grad, axis=1, keepdims=True) * (
+                1.0 / width
+            )
+            row_state[half] = total
+            rows[half] = rows[half] - rows_grad * (0.1 * lax.rsqrt(total))
+            if not last:
                 round_rows(half)
 
     for load in small_loads:

time: 59 us -> 59 us (level)
  no operation moved by 1% of the time
where the time goes in v10:
time: 59 us; the launch traced here: 58.8 us
  Pallas kernels  58.1 us (98%)
  between operations  0.64 us (1%)
    pallas_call x1, Pallas kernels, body(): pl.pallas_call(functools.partial(kernel, n_outer, n_inner), out_shape=tup...  56.8 us
    pallas_call x1, Pallas kernels, body(): pl.pallas_call(store_kernel, out_shape=tuple((jax.ShapeDtypeStruct(shape,...  1.37 us

profile of v10, /device:TPU:0, one launch (start us, length us, event | category | flops | bytes accessed | tf_op | source)
XLA Modules:
  0.0 58.8 jit_solution(2421206961095937003)
XLA Ops:
  0.6 56.8 %shard_map.93 = (f32[256,1024]{1,0:T(8,128)S(1)}, f32[1,256]{1,0:T(1,128)S(1)}, f32[8,32,1024]{2,1,0:T(8,128)S(1)}, f32[1,256]{1,0:T(1,128)S(1)}) custom-call(f32[256,1024]{1,0:T(8,128)} %vertex.1, f32[1,256]{1,0:T(1,128)} %bitcast.8, f32[8,32,1024]{2,1,0:T(8,128)} %bitcast.6, f32[1,256]{1,0:T(1,128)} %bitcast.9, s32[1,1536]{1,0:T(1,128)} %edge_source_in.1, ...), custom_call_target="tpu_custom_call" | custom-call | flops 1409286144 | bytes 4194304 | tf_op jit(solution)/shard_map/pallas_call | solution.py:314
  57.4 1.4 %shard_map.94 = (f32[256,1024]{1,0:T(8,128)}, f32[1,256]{1,0:T(1,128)}, f32[8,32,1024]{2,1,0:T(8,128)}, f32[1,256]{1,0:T(1,128)}) custom-call(f32[256,1024]{1,0:T(8,128)S(1)} %get-tuple-element.12.refs_0_, f32[1,256]{1,0:T(1,128)S(1)} %get-tuple-element.13.refs_1_, f32[8,32,1024]{2,1,0:T(8,128)S(1)} %get-tuple-element.14.refs_2_, ...), custom_call_target="tpu_custom_call" | custom-call | tf_op jit(solution)/shard_map/pallas_call | solution.py:354
